TPU v7x, 32 devices: a whole 2x2x4 slice. The times are simulated.
32 devices in a mesh: groups: 2 (over y), grid: 4 (over z), head: 4 (over x, core).
Axes of the slice: x: 2, y: 2, z: 4, core: 2. Of those that a mesh axis runs over, the one named last changes fastest.
Arguments:
- queries: bfloat16 [64, 4096], P(('groups', 'grid', 'head')), parts along dimension 0, may hold values from -200 to 200
- cache_keys: bfloat16 [4, 8192, 512], P('groups', 'grid', 'head'), parts along dimension 0, may hold values from -6 to 6
- cache_values: bfloat16 [4, 8192, 512], P('groups', 'grid', 'head'), parts along dimension 0, may hold values from -96 to 96
- stretch_keys: bfloat16 [64, 512], P(('groups', 'grid', 'head')), parts along dimension 0, may hold values from -9 to 9
- stretch_values: bfloat16 [64, 512], P(('groups', 'grid', 'head')), parts along dimension 0, may hold values from -96 to 96
- cache_lengths: int32 [4], P('groups'), parts along dimension 0, may hold values from 1024 to 8192, as said below
Outputs:
- attended: bfloat16 [64, 4096], P(('groups', 'grid'), 'head'), parts along dimension 0
There are 2 independent parts, one for each index of `groups`. A program takes and returns all parts, laid end to end along the dimension named above; each array names one. Nothing has to cross between parts.
Inputs may be any that keep to these rules, and one draw needn't show every extreme that they name: `cache_lengths`: in every group some request has cache length exactly 8192.
All inputs are finite; a program needn't handle non-finite values.
Results may differ from a plain program's by a relative error of at most 0.0085.
Values may be sent and summed in bfloat16 or wider, within the bound.
A program may use at most 64 MiB of HBM per device.

v0:
```python
import math

import jax
import jax.numpy as jnp
from jax import lax
from jax.sharding import PartitionSpec as P

HD = 128
GROUP = 8
REQS = 2


NEG = -1e30


def cache_terms(query, keys, values, visible, floor):
    scores = jnp.einsum("qd,kd->qk", query, keys, preferred_element_type=jnp.float32) * (
        1.0 / math.sqrt(HD)
    )
    top = jnp.maximum(floor, jnp.max(jnp.where(visible, scores, NEG), axis=1))
    weights = jnp.where(visible, jnp.exp(scores - top[:, None]), 0.0).astype(jnp.bfloat16)
    total = jnp.sum(weights.astype(jnp.float32), axis=1)
    summed = jnp.dot(weights, values, preferred_element_type=jnp.float32)
    return (top, total, summed)


def shards(queries, cache_keys, cache_values, stretch_keys, stretch_values, cache_lengths):
    mine_q, mine_k, mine_v = (
        lax.all_to_all(queries, "head", split_axis=1, concat_axis=0, tiled=True),
        lax.all_to_all(stretch_keys, "head", split_axis=1, concat_axis=0, tiled=True),
        lax.all_to_all(stretch_values, "head", split_axis=1, concat_axis=0, tiled=True),
    )
    all_q = lax.all_gather(mine_q, "grid", axis=0, tiled=True)
    stretch = all_q.shape[0]
    own_rows = mine_q.shape[0]
    span = cache_keys.shape[1]
    per_req = stretch // REQS
    place = lax.axis_index("grid")
    key_pos = place * span + lax.iota(jnp.int32, span)
    stretch_pos = place * own_rows + lax.iota(jnp.int32, own_rows)
    scale = 1.0 / math.sqrt(HD)
    request_rows = per_req * GROUP
    block_rows = min(512, request_rows)
    blocks = request_rows // block_rows
    tops, totals, sums = ([], [], [])
    for request in range(REQS):
        keys = cache_keys[request]
        values = cache_values[request]
        length = cache_lengths[request]
        far = (key_pos < length)[None, :]
        query_all = all_q[request * per_req : (request + 1) * per_req].reshape(
            blocks, block_rows, HD
        )
        pos_all = (request * per_req + lax.iota(jnp.int32, request_rows) // GROUP).reshape(
            blocks, block_rows
        )

        def one_block(items):
            query, query_pos = items
            near = (stretch_pos[None, :] // per_req == request) & (
                stretch_pos[None, :] <= query_pos[:, None]
            )
            near_scores = (
                jnp.einsum("qd,kd->qk", query, mine_k, preferred_element_type=jnp.float32) * scale
            )
            near_top = jnp.maximum(NEG, jnp.max(jnp.where(near, near_scores, NEG), axis=1))
            top, total, summed = cache_terms(query, keys, values, far, near_top)
            near_w = jnp.where(near, jnp.exp(near_scores - top[:, None]), 0.0).astype(jnp.bfloat16)
            total = total + jnp.sum(near_w.astype(jnp.float32), axis=1)
            summed = summed + jnp.dot(near_w, mine_v, preferred_element_type=jnp.float32)
            return (top, total, summed)

        top, total, summed = lax.map(one_block, (query_all, pos_all))
        tops.append(top.reshape(per_req, GROUP))
        totals.append(total.reshape(per_req, GROUP))
        sums.append(summed.reshape(per_req, GROUP, HD))
    tops = jnp.concatenate(tops, 0)
    totals = jnp.concatenate(totals, 0)
    sums = jnp.concatenate(sums, 0)
    outputs = (sums / jnp.maximum(totals, 1.0)[..., None]).astype(jnp.bfloat16)
    width = lax.axis_size("grid")
    share = stretch // width
    got_top, got_total = (
        lax.all_to_all(
            tops.reshape(width, share, GROUP), "grid", split_axis=0, concat_axis=0, tiled=True
        ),
        lax.all_to_all(
            totals.reshape(width, share, GROUP), "grid", split_axis=0, concat_axis=0, tiled=True
        ),
    )
    got_out = lax.all_to_all(
        outputs.reshape(width, share, GROUP * HD), "grid", split_axis=0, concat_axis=0, tiled=True
    )
    peak = jnp.max(got_top, axis=0)
    factor = jnp.exp(got_top - peak[None]) * got_total
    total = jnp.sum(factor, axis=0)
    summed = jnp.sum(
        got_out.reshape(width, share, GROUP, HD).astype(jnp.float32) * factor[..., None], axis=0
    )
    return (summed / total[..., None]).reshape(-1, GROUP * HD).astype(jnp.bfloat16)


def solution(mesh):
    in_specs = (
        P(("groups", "grid", "head"), None),
        P("groups", "grid", "head"),
        P("groups", "grid", "head"),
        P(("groups", "grid", "head"), None),
        P(("groups", "grid", "head"), None),
        P("groups"),
    )
    out_specs = P(("groups", "grid"), "head")
    return jax.shard_map(shards, mesh=mesh, in_specs=in_specs, out_specs=out_specs, check_vma=False)
```

profile of v0, /device:TPU:0, one launch (start us, length us, event | category | flops | bytes accessed | tf_op | source)
XLA Modules:
  0.0 63.4 jit_solution(4845166243577330291)
XLA Ops:
  0.0 4.2 %all-to-all-start = ((bf16[2,4,1024]{2,0,1:T(2,128)(2,1)}), bf16[2,4,1024]{2,0,1:T(2,128)(2,1)S(1)}, u32[]{:S(2)}, u32[]{:S(2)}) async-start(bf16[2,4,1024]{2,0,1:T(2,128)(2,1)} %bitcast.55), calls=%async_computation | async-start | bytes 32768 | tf_op jit(solution)/shard_map/all_to_all | solution.py:29
  4.2 0.0 copy-start.1
  4.2 0.6 %copy-done.1 = s32[2]{0:T(128)S(1)} copy-done((s32[2]{0:T(128)S(1)}, s32[2]{0:T(128)}, u32[]{:S(2)}) %copy-start.1) | copy-done | bytes 32
  4.9 0.7 %fusion.19 = (s32[1]{0:T(128)}, s32[1]{0:T(128)}) fusion(s32[2]{0:T(128)S(1)} %copy-done.1), kind=kLoop, calls=%fused_computation.61 | loop fusion | bytes 16 | tf_op jit(solution)/shard_map/slice | solution.py:49
  5.5 1.3 %fusion.15 = (pred[2048]{0:T(1024)(128)(4,1)S(1)}, pred[2048]{0:T(1024)(128)(4,1)S(1)}) fusion(s32[]{:T(128)} %bitcast.12, s32[]{:T(128)S(6)} %mul.36, s32[]{:T(128)} %bitcast), kind=kLoop, calls=%fused_computation.32 | loop fusion | flops 6144 | bytes 4108 | tf_op jit(solution)/shard_map/lt | solution.py:50
  6.9 1.2 %all-to-all-done = bf16[2,4,1024]{2,0,1:T(2,128)(2,1)S(1)} async-done(((bf16[2,4,1024]{2,0,1:T(2,128)(2,1)}), bf16[2,4,1024]{2,0,1:T(2,128)(2,1)S(1)}, u32[]{:S(2)}, u32[]{:S(2)}) %all-to-all-start) | async-done | bytes 16416 | tf_op jit(solution)/shard_map/all_to_all | solution.py:29
  8.1 3.2 %all-to-all-start.1 = ((bf16[2,4,128]{2,0,1:T(2,128)(2,1)}), bf16[2,4,128]{2,0,1:T(2,128)(2,1)S(1)}, u32[]{:S(2)}, u32[]{:S(2)}) async-start(bf16[2,4,128]{2,0,1:T(2,128)(2,1)} %bitcast.4), calls=%async_computation.1 | async-start | bytes 4096 | tf_op jit(solution)/shard_map/all_to_all | solution.py:30
  11.3 13.8 %all_gather.3 = bf16[32,1024]{1,0:T(8,128)(2,1)S(1)} all-gather(bf16[8,1024]{1,0:T(8,128)(2,1)S(1)} %all_to_all.54), channel_id=1, replica_groups=mesh['groups'=2,'grid'=4,'head'=4] {'grid'}, dimensions={0}, use_global_device_ids=true | all-gather | bytes 81920 | tf_op jit(solution)/shard_map/all_gather | solution.py:33
  25.2 0.0 all-to-all-done.1
  25.2 3.3 %all-to-all-start.2 = ((bf16[2,4,128]{2,0,1:T(2,128)(2,1)}), bf16[2,4,128]{2,0,1:T(2,128)(2,1)S(1)}, u32[]{:S(2)}, u32[]{:S(2)}) async-start(bf16[2,4,128]{2,0,1:T(2,128)(2,1)} %bitcast.8), calls=%async_computation.2 | async-start | bytes 4096 | tf_op jit(solution)/shard_map/all_to_all | solution.py:31
  28.5 0.1 convolution_multiply_fusion.2
  28.7 0.0 copy-start.2
  28.7 1.5 %select_reduce_fusion.1 = (f32[128]{0:T(128)S(1)}, f32[128,2048]{1,0:T(8,128)S(1)}) fusion(pred[2048]{0:T(1024)(128)(4,1)S(1)} %get-tuple-element.98, bf16[128,128]{1,0:T(8,128)(2,1)S(1)} %squeeze.33, bf16[2,2048,128]{2,1,0:T(8,128)(2,1)} %param.7), kind=kOutput, calls=%fused_computation.13 | convolution fusion | flops 67895168 | bytes 1608192 | tf_op jit(solution)/shard_map/while/body/eval_jaxpr/qd,kd->qk/dot_general | solution.py:17
  30.2 0.1 select_reduce_fusion.3
  30.4 0.1 max.60
  30.4 0.3 convert_reduce_fusion.1
  30.8 0.0 copy-done.2
  30.8 0.0 copy-start
  30.8 0.4 fusion.5
  31.2 0.8 %copy-done = bf16[2,2048,128]{2,1,0:T(8,128)(2,1)S(1)} copy-done((bf16[2,2048,128]{2,1,0:T(8,128)(2,1)S(1)}, bf16[2,2048,128]{2,1,0:T(8,128)(2,1)}, u32[]{:S(2)}) %copy-start) | copy-done | bytes 1048600
  32.0 0.4 select_reduce_fusion
  32.4 0.3 convert_reduce_fusion
  32.8 0.4 fusion.2
  33.1 0.1 max.61
  33.2 0.1 copy.18
  33.3 0.1 convert_reduce_fusion.3
  33.4 0.1 copy.19
  33.4 0.1 pad_maximum_fusion.1
  33.5 0.1 add.88
  33.6 0.1 copy.16
  33.7 0.1 add.86
  33.8 0.1 copy.15
  33.8 0.7 %copy.24 = f32[32,8]{1,0:T(8,128)} copy(f32[32,8]{0,1:T(8,128)S(1)} %pad_maximum_fusion.1) | data formatting | bytes 2048 | tf_op jit(solution)/shard_map/reshape | solution.py:85
  34.5 0.0 all-to-all-done.2
  34.5 4.6 %all-to-all-start.4 = ((f32[4,8,8]{2,1,0:T(8,128)}), f32[4,8,8]{2,1,0:T(8,128)S(1)}, u32[]{:S(2)}, u32[]{:S(2)}) async-start(f32[4,8,8]{2,1,0:T(8,128)} %bitcast.18), calls=%async_computation.4 | async-start | bytes 32768 | tf_op jit(solution)/shard_map/all_to_all | solution.py:84
  39.1 0.2 fusion.1
  39.3 0.2 fusion
  39.6 0.1 broadcast_maximum_fusion
  39.6 0.1 copy.17
  39.7 0.7 %copy.25 = f32[32,8]{1,0:T(8,128)} copy(f32[32,8]{0,1:T(8,128)S(1)} %get-tuple-element.56) | data formatting | bytes 2048 | tf_op jit(solution)/shard_map/reshape | solution.py:88
  40.4 4.3 %all-to-all-done.4 = f32[4,8,8]{2,1,0:T(8,128)S(1)} async-done(((f32[4,8,8]{2,1,0:T(8,128)}), f32[4,8,8]{2,1,0:T(8,128)S(1)}, u32[]{:S(2)}, u32[]{:S(2)}) %all-to-all-start.4) | async-done | bytes 1056 | tf_op jit(solution)/shard_map/all_to_all | solution.py:84
  44.7 3.3 %all-to-all-start.5 = ((f32[4,8,8]{2,1,0:T(8,128)}), f32[4,8,8]{2,1,0:T(8,128)S(1)}, u32[]{:S(2)}, u32[]{:S(2)}) async-start(f32[4,8,8]{2,1,0:T(8,128)} %bitcast.19), calls=%async_computation.5 | async-start | bytes 32768 | tf_op jit(solution)/shard_map/all_to_all | solution.py:87
  48.0 0.1 fusion.12
  48.1 0.7 %convert_element_type.55 = bf16[4,8,1024]{2,1,0:T(8,128)(2,1)} reshape(bf16[32,8,128]{2,1,0:T(8,128)(2,1)S(1)} %fusion.12) | data formatting | bytes 131072 | tf_op jit(solution)/shard_map/convert_element_type | solution.py:80
  48.8 4.8 %all-to-all-done.5 = f32[4,8,8]{2,1,0:T(8,128)S(1)} async-done(((f32[4,8,8]{2,1,0:T(8,128)}), f32[4,8,8]{2,1,0:T(8,128)S(1)}, u32[]{:S(2)}, u32[]{:S(2)}) %all-to-all-start.5) | async-done | bytes 1056 | tf_op jit(solution)/shard_map/all_to_all | solution.py:87
  53.6 3.3 %all-to-all-start.3 = ((bf16[4,8,1024]{2,1,0:T(8,128)(2,1)}), bf16[4,8,1024]{2,1,0:T(8,128)(2,1)S(1)}, u32[]{:S(2)}, u32[]{:S(2)}) async-start(bf16[4,8,1024]{2,1,0:T(8,128)(2,1)} %convert_element_type.55), calls=%async_computation.3 | async-start | bytes 131072 | tf_op jit(solution)/shard_map/all_to_all | solution.py:91
  56.9 0.1 copy.23
  57.0 0.1 copy.22
  57.0 5.5 %all-to-all-done.3 = bf16[4,8,1024]{2,1,0:T(8,128)(2,1)S(1)} async-done(((bf16[4,8,1024]{2,1,0:T(8,128)(2,1)}), bf16[4,8,1024]{2,1,0:T(8,128)(2,1)S(1)}, u32[]{:S(2)}, u32[]{:S(2)}) %all-to-all-start.3) | async-done | bytes 65568 | tf_op jit(solution)/shard_map/all_to_all | solution.py:91
  62.6 0.1 fusion.13
  62.7 0.7 %fusion.14 = bf16[8,1024]{1,0:T(8,128)(2,1)} fusion(f32[8,1024]{1,0:T(8,128)S(1)} %fusion.13, f32[8,8]{0,1:T(8,128)S(1)} %copy.23), kind=kLoop, calls=%fused_computation.29 | loop fusion | flops 16384 | bytes 49408 | tf_op jit(solution)/shard_map/convert_element_type | solution.py:100
  (13 shorter events, 0.1 us)
Async XLA Ops:
  0.0 8.1 %all-to-all-start = ((bf16[2,4,1024]{2,0,1:T(2,128)(2,1)}), bf16[2,4,1024]{2,0,1:T(2,128)(2,1)S(1)}, u32[]{:S(2)}, u32[]{:S(2)}) async-start(bf16[2,4,1024]{2,0,1:T(2,128)(2,1)} %bitcast.55), calls=%async_computation | async-start | bytes 32768 | tf_op jit(solution)/shard_map/all_to_all | solution.py:29
  4.2 0.7 %copy-start.1 = (s32[2]{0:T(128)S(1)}, s32[2]{0:T(128)}, u32[]{:S(2)}) copy-start(s32[2]{0:T(128)} %param.11) | copy-start | bytes 28
  8.1 17.1 %all-to-all-start.1 = ((bf16[2,4,128]{2,0,1:T(2,128)(2,1)}), bf16[2,4,128]{2,0,1:T(2,128)(2,1)S(1)}, u32[]{:S(2)}, u32[]{:S(2)}) async-start(bf16[2,4,128]{2,0,1:T(2,128)(2,1)} %bitcast.4), calls=%async_computation.1 | async-start | bytes 4096 | tf_op jit(solution)/shard_map/all_to_all | solution.py:30
  25.2 9.3 %all-to-all-start.2 = ((bf16[2,4,128]{2,0,1:T(2,128)(2,1)}), bf16[2,4,128]{2,0,1:T(2,128)(2,1)S(1)}, u32[]{:S(2)}, u32[]{:S(2)}) async-start(bf16[2,4,128]{2,0,1:T(2,128)(2,1)} %bitcast.8), calls=%async_computation.2 | async-start | bytes 4096 | tf_op jit(solution)/shard_map/all_to_all | solution.py:31
  28.7 2.1 %copy-start.2 = (bf16[2,2048,128]{2,1,0:T(8,128)(2,1)S(1)}, bf16[2,2048,128]{2,1,0:T(8,128)(2,1)}, u32[]{:S(2)}) copy-start(bf16[2,2048,128]{2,1,0:T(8,128)(2,1)} %param.8) | copy-start | bytes 3145732
  30.8 1.2 %copy-start = (bf16[2,2048,128]{2,1,0:T(8,128)(2,1)S(1)}, bf16[2,2048,128]{2,1,0:T(8,128)(2,1)}, u32[]{:S(2)}) copy-start(bf16[2,2048,128]{2,1,0:T(8,128)(2,1)} %param.7) | copy-start | bytes 3145732
  34.5 10.2 %all-to-all-start.4 = ((f32[4,8,8]{2,1,0:T(8,128)}), f32[4,8,8]{2,1,0:T(8,128)S(1)}, u32[]{:S(2)}, u32[]{:S(2)}) async-start(f32[4,8,8]{2,1,0:T(8,128)} %bitcast.18), calls=%async_computation.4 | async-start | bytes 32768 | tf_op jit(solution)/shard_map/all_to_all | solution.py:84
  44.7 8.8 %all-to-all-start.5 = ((f32[4,8,8]{2,1,0:T(8,128)}), f32[4,8,8]{2,1,0:T(8,128)S(1)}, u32[]{:S(2)}, u32[]{:S(2)}) async-start(f32[4,8,8]{2,1,0:T(8,128)} %bitcast.19), calls=%async_computation.5 | async-start | bytes 32768 | tf_op jit(solution)/shard_map/all_to_all | solution.py:87
  53.6 9.0 %all-to-all-start.3 = ((bf16[4,8,1024]{2,1,0:T(8,128)(2,1)}), bf16[4,8,1024]{2,1,0:T(8,128)(2,1)S(1)}, u32[]{:S(2)}, u32[]{:S(2)}) async-start(bf16[4,8,1024]{2,1,0:T(8,128)(2,1)} %convert_element_type.55), calls=%async_computation.3 | async-start | bytes 131072 | tf_op jit(solution)/shard_map/all_to_all | solution.py:91
where the time goes:
time: 64 us; the launch traced here: 63.4 us
  starting transfers between devices  21.9 us (34%)
  waiting for transfers between devices  15.9 us (25%)
  blocking collectives  13.8 us (22%)
  local copies, waits for them, and re-layouts  5.06 us (8%)
  matrix products  3.35 us (5%)
  other arithmetic  3.23 us (5%)
    all_gather x1, blocking collectives, shards(): all_q = lax.all_gather(mine_q, 'grid', axis=0, tiled=True)  13.8 us
    all_to_all x1, waiting for transfers between devices, shards(): lax.all_to_all(outputs.reshape(width, share, GROUP * HD), 'grid', split_a...  5.55 us
    all_to_all x1, waiting for transfers between devices, shards(): lax.all_to_all(totals.reshape(width, share, GROUP), 'grid', split_axis=0,...  4.8 us
    all_to_all x1, starting transfers between devices, shards(): lax.all_to_all(tops.reshape(width, share, GROUP), 'grid', split_axis=0, c...  4.59 us
    all_to_all x1, waiting for transfers between devices, shards(): lax.all_to_all(tops.reshape(width, share, GROUP), 'grid', split_axis=0, c...  4.34 us
    all_to_all x1, starting transfers between devices, shards(): lax.all_to_all(queries, 'head', split_axis=1, concat_axis=0, tiled=True)  4.21 us
    all_to_all x1, starting transfers between devices, shards(): lax.all_to_all(stretch_values, 'head', split_axis=1, concat_axis=0, tiled...  3.33 us
    all_to_all x1, starting transfers between devices, shards(): lax.all_to_all(outputs.reshape(width, share, GROUP * HD), 'grid', split_a...  3.28 us
  transfers between devices with their start and end apart: 6, of which 4 were waited for; matrix products, arithmetic and copies ran while one was open for 15% of the time, Pallas kernels for 0%

commit v1 on v0

v1 whole, which is shorter than its diff:
```python
import functools
import math

import jax
import jax.numpy as jnp
from jax import lax
from jax.experimental import pallas as pl
from jax.experimental.pallas import tpu as pltpu
from jax.sharding import PartitionSpec as P

HD = 128
GROUP = 8
REQS = 2
PAD = 16
BLOCK_SRC = 8

MASKED = -1e30
FLOOR = -1e29
LOG2_SCALE = math.log2(math.e) / math.sqrt(HD)

MESH = pl.DeviceIdType.MESH
F32 = jnp.float32
BF16 = jnp.bfloat16


def repeat(start, stop, body):
    if stop - start <= 16:
        for i in range(start, stop):
            body(i)
    else:

        def step(i, carry):
            body(i)
            return carry

        lax.fori_loop(start, stop, step, 0)


def attend(query, keys, values, near_keys, near_values, bias, near_seen):
    contract = (((1,), (1,)), ((), ()))
    scores = lax.dot_general(query, keys, contract, preferred_element_type=F32) + bias
    near = lax.dot_general(query, near_keys, contract, preferred_element_type=F32)
    near = jnp.where(near_seen, near, MASKED)
    top = jnp.maximum(jnp.max(scores, axis=1, keepdims=True), jnp.max(near, axis=1, keepdims=True))
    top = jnp.maximum(top, FLOOR)
    weights = jnp.exp2((scores - top) * LOG2_SCALE)
    near_w = jnp.exp2((near - top) * LOG2_SCALE)
    total = jnp.sum(weights, axis=1, keepdims=True) + jnp.sum(near_w, axis=1, keepdims=True)
    summed = jnp.dot(weights.astype(BF16), values, preferred_element_type=F32)
    summed = summed + jnp.dot(near_w.astype(BF16), near_values, preferred_element_type=F32)
    return top, total, summed


def kernel(
    nz, nh,
    q_in, k_in, v_in, sk_in, sv_in, len_in,
    out_ref,
    q_own, sk_own, sv_own, lens, keys, values,
    q_pack, kv_pack, q_msg, kv_msg, q_all, kv_all,
    sum_msg, stat_msg, sum_all, stat_all, merged,
    load_sem, cache_sem, q_send, q_recv, kv_send, kv_recv, sum_send, sum_recv, stat_send, stat_recv,
):
    n = nz * nh
    z, h = lax.axis_index("grid"), lax.axis_index("head")
    me = z * nh + h
    local_rows = q_own.shape[0]
    msg_rows = local_rows * GROUP
    span = keys.shape[1]
    own_rows = local_rows * nh
    per_req = own_rows * nz // REQS
    owner_rows = own_rows * GROUP
    block_rows = BLOCK_SRC * msg_rows
    blocks = n // BLOCK_SRC
    owners = block_rows // owner_rows

    def peer(k):
        other = lax.rem(me + k, n)
        return other // nh, lax.rem(other, nh)

    barrier = pltpu.get_barrier_semaphore()

    def greet(k):
        oz, oh = peer(k)
        pl.semaphore_signal(barrier, inc=1, device_id={"grid": oz, "head": oh}, device_id_type=MESH)

    repeat(1, n, greet)

    loads = [
        pltpu.make_async_copy(q_in, q_own, load_sem.at[0]),
        pltpu.make_async_copy(sk_in, sk_own, load_sem.at[1]),
        pltpu.make_async_copy(sv_in, sv_own, load_sem.at[2]),
        pltpu.make_async_copy(len_in, lens, load_sem.at[3]),
    ]
    for load in loads:
        load.start()
    cache_loads = []
    for r in range(REQS):
        pair = (
            pltpu.make_async_copy(k_in.at[r], keys.at[r], cache_sem.at[2 * r]),
            pltpu.make_async_copy(v_in.at[r], values.at[r], cache_sem.at[2 * r + 1]),
        )
        for load in pair:
            load.start()
        cache_loads.append(pair)

    kv_pack[...] = jnp.zeros_like(kv_pack)
    kv_all[nh:] = jnp.zeros((kv_all.shape[0] - nh,) + kv_all.shape[1:], BF16)
    loads[0].wait()
    q32 = q_own[...].astype(F32)
    for oh in range(nh):
        for j in range(GROUP):
            column = (oh * GROUP + j) * HD
            q_pack[pl.ds(oh * msg_rows + j, local_rows, stride=GROUP), :] = q32[:, column : column + HD]
    q_msg[...] = q_pack[...].astype(BF16).reshape(q_msg.shape)
    loads[1].wait()
    loads[2].wait()
    for t, own in enumerate((sk_own, sv_own)):
        own32 = own[...].astype(F32)
        for oh in range(nh):
            kv_pack[pl.ds((oh * 2 + t) * PAD, local_rows), :] = own32[:, oh * HD : (oh + 1) * HD]
    kv_msg[...] = kv_pack[...].astype(BF16).reshape(kv_msg.shape)

    pl.semaphore_wait(barrier, n - 1)

    def send_q(k):
        oz, oh = peer(k)
        pltpu.make_async_remote_copy(
            src_ref=q_msg.at[oh], dst_ref=q_all.at[me], send_sem=q_send, recv_sem=q_recv.at[me // BLOCK_SRC],
            device_id={"grid": oz, "head": oh}, device_id_type=MESH,
        ).start()

    repeat(1, n, send_q)
    pltpu.make_async_copy(q_msg.at[h], q_all.at[me], q_recv.at[me // BLOCK_SRC]).start()
    for k in range(1, nh):
        oh = lax.rem(h + k, nh)
        pltpu.make_async_remote_copy(
            src_ref=kv_msg.at[oh], dst_ref=kv_all.at[h], send_sem=kv_send, recv_sem=kv_recv,
            device_id={"grid": z, "head": oh}, device_id_type=MESH,
        ).start()
    pltpu.make_async_copy(kv_msg.at[h], kv_all.at[h], kv_recv).start()

    loads[3].wait()
    unrolled = blocks <= 4
    if not unrolled:
        for pair in cache_loads:
            for load in pair:
                load.wait()
    landed = kv_all.at[pl.ds(0, nh)]
    pltpu.make_async_copy(landed, landed, kv_recv).wait()
    near_cols = kv_all.shape[0] * PAD
    near_keys = kv_all[:, 0].reshape(near_cols, HD)
    near_values = kv_all[:, 1].reshape(near_cols, HD)
    key_pos = z * span + lax.broadcasted_iota(jnp.int32, (1, span), 1)
    col = lax.broadcasted_iota(jnp.int32, (block_rows, near_cols), 1)
    row = lax.broadcasted_iota(jnp.int32, (block_rows, near_cols), 0)
    near_pos = z * own_rows + (col // PAD) * local_rows + col % PAD
    near_real = (col % PAD < local_rows) & (col < nh * PAD)
    owner_row = lax.broadcasted_iota(jnp.int32, (owner_rows, 128), 0)
    owner_lane = lax.broadcasted_iota(jnp.int32, (owner_rows, 128), 1)
    diagonal = owner_lane % owner_rows == owner_row

    def one_block(blk):
        first_row = blk * (block_rows // GROUP)
        request = first_row // per_req
        sources = pl.ds(blk * BLOCK_SRC, BLOCK_SRC)
        if unrolled and first_row % per_req == 0:
            for load in cache_loads[request]:
                load.wait()
        pltpu.make_async_copy(q_all.at[sources], q_all.at[sources], q_recv.at[blk]).wait()
        query = q_all[sources].reshape(block_rows, HD)
        bias = jnp.where(key_pos < lens[request], 0.0, MASKED)
        near_seen = near_real & (near_pos // per_req == request) & (near_pos <= first_row + row // GROUP)
        top, total, summed = attend(query, keys[request], values[request], near_keys, near_values, bias, near_seen)
        summed = summed.astype(BF16)
        for o in range(owners):
            owner = blk * owners + o
            part = slice(o * owner_rows, (o + 1) * owner_rows)
            sum_msg[owner] = summed[part]
            for t, stat in enumerate((top, total)):
                stat_msg[owner, t : t + 1, :] = jnp.sum(
                    jnp.where(diagonal, stat[part], 0.0), axis=0, keepdims=True
                )

            @pl.when(owner != z)
            def _():
                pltpu.make_async_remote_copy(
                    src_ref=stat_msg.at[owner], dst_ref=stat_all.at[z], send_sem=stat_send, recv_sem=stat_recv,
                    device_id={"grid": owner, "head": h}, device_id_type=MESH,
                ).start()
                pltpu.make_async_remote_copy(
                    src_ref=sum_msg.at[owner], dst_ref=sum_all.at[z], send_sem=sum_send, recv_sem=sum_recv,
                    device_id={"grid": owner, "head": h}, device_id_type=MESH,
                ).start()

            @pl.when(owner == z)
            def _():
                pltpu.make_async_copy(stat_msg.at[owner], stat_all.at[z], stat_recv).start()
                pltpu.make_async_copy(sum_msg.at[owner], sum_all.at[z], sum_recv).start()

    if unrolled:
        for blk in range(blocks):
            one_block(blk)
    else:
        repeat(0, blocks, one_block)

    pltpu.make_async_copy(stat_all, stat_all, stat_recv).wait()
    tops = [stat_all[b, 0:1, :] for b in range(nz)]
    peak = functools.reduce(jnp.maximum, tops)
    shares = [jnp.exp2((top - peak) * LOG2_SCALE) for top in tops]
    total = sum(share * stat_all[b, 1:2, :] for b, share in enumerate(shares))
    shares = [share / total for share in shares]
    per_tile = 128 // owner_rows
    pltpu.make_async_copy(sum_all, sum_all, sum_recv).wait()
    acc = jnp.zeros((owner_rows, HD), F32)
    for b in range(0, nz, per_tile):
        share = shares[b]
        for o in range(1, per_tile):
            share = jnp.where(owner_lane >= o * owner_rows, shares[b + o], share)
        mix = jnp.where(diagonal, share, 0.0)
        high = mix.astype(BF16)
        low = (mix - high.astype(F32)).astype(BF16)
        sums = sum_all[pl.ds(b, per_tile)].reshape(per_tile * owner_rows, HD)
        acc = acc + jnp.dot(high, sums, preferred_element_type=F32)
        acc = acc + jnp.dot(low, sums, preferred_element_type=F32)
    merged[...] = acc
    for j in range(GROUP):
        out_ref[:, j * HD : (j + 1) * HD] = merged[pl.ds(j, own_rows, stride=GROUP), :].astype(BF16)

    sent = q_all.at[pl.ds(0, n - 1)]
    pltpu.make_async_copy(sent, sent, q_send).wait()
    sent = kv_all.at[pl.ds(0, nh - 1)]
    pltpu.make_async_copy(sent, sent, kv_send).wait()
    sent = stat_all.at[pl.ds(0, nz - 1)]
    pltpu.make_async_copy(sent, sent, stat_send).wait()
    sent = sum_all.at[pl.ds(0, nz - 1)]
    pltpu.make_async_copy(sent, sent, sum_send).wait()


def shards(queries, cache_keys, cache_values, stretch_keys, stretch_values, cache_lengths):
    nz, nh = lax.axis_size("grid"), lax.axis_size("head")
    n = nz * nh
    local_rows = queries.shape[0]
    msg_rows = local_rows * GROUP
    owner_rows = local_rows * nh * GROUP
    slots = -(-nh * PAD // 128) * 128 // PAD
    any_spec = pl.BlockSpec(memory_space=pl.ANY)
    vmem_spec = pl.BlockSpec(memory_space=pltpu.VMEM)
    dma = pltpu.SemaphoreType.DMA
    return pl.pallas_call(
        functools.partial(kernel, nz, nh),
        out_shape=jax.ShapeDtypeStruct((local_rows * nh, GROUP * HD), BF16),
        in_specs=[any_spec] * 6,
        out_specs=vmem_spec,
        scratch_shapes=[
            pltpu.VMEM(queries.shape, BF16),
            pltpu.VMEM(stretch_keys.shape, BF16),
            pltpu.VMEM(stretch_values.shape, BF16),
            pltpu.SMEM(cache_lengths.shape, jnp.int32),
            pltpu.VMEM(cache_keys.shape, BF16),
            pltpu.VMEM(cache_values.shape, BF16),
            pltpu.VMEM((nh * msg_rows, HD), F32),
            pltpu.VMEM((nh * 2 * PAD, HD), F32),
            pltpu.VMEM((nh, msg_rows, HD), BF16),
            pltpu.VMEM((nh, 2, PAD, HD), BF16),
            pltpu.VMEM((n, msg_rows, HD), BF16),
            pltpu.VMEM((slots, 2, PAD, HD), BF16),
            pltpu.VMEM((nz, owner_rows, HD), BF16),
            pltpu.VMEM((nz, 2, 128), F32),
            pltpu.VMEM((nz, owner_rows, HD), BF16),
            pltpu.VMEM((nz, 2, 128), F32),
            pltpu.VMEM((owner_rows, HD), F32),
            dma((4,)),
            dma((2 * REQS,)),
            dma,
            dma((n // BLOCK_SRC,)),
            dma,
            dma,
            dma,
            dma,
            dma,
            dma,
        ],
        compiler_params=pltpu.CompilerParams(
            collective_id=0, has_side_effects=True, vmem_limit_bytes=48 * 1024 * 1024
        ),
    )(queries, cache_keys, cache_values, stretch_keys, stretch_values, cache_lengths)


def solution(mesh):
    in_specs = (
        P(("groups", "grid", "head"), None),
        P("groups", "grid", "head"),
        P("groups", "grid", "head"),
        P(("groups", "grid", "head"), None),
        P(("groups", "grid", "head"), None),
        P("groups"),
    )
    out_specs = P(("groups", "grid"), "head")
    return jax.shard_map(shards, mesh=mesh, in_specs=in_specs, out_specs=out_specs, check_vma=False)
```

time: 64 us -> 20.7 us (0.32)
  starting transfers between devices: 21.9 us -> 0 us
  waiting for transfers between devices: 15.9 us -> 0 us
  Pallas kernels: 0 us -> 14.6 us
  blocking collectives: 13.8 us -> 0 us
  matrix products: 3.35 us -> 0 us
  other arithmetic: 3.23 us -> 0 us
  local copies, waits for them, and re-layouts: 5.06 us -> 5.79 us
    all_to_all x6 -> x0, starting transfers between devices: 21.9 us -> none  [the longest x1 4.59 us: shards(): lax.all_to_all(tops.reshape(width, share, GROUP), 'grid', split_axis=0, c...]
    all_to_all x6 -> x0, waiting for transfers between devices: 15.9 us -> none  [the longest x1 5.55 us: shards(): lax.all_to_all(outputs.reshape(width, share, GROUP * HD), 'grid', split_a...]
    pallas_call x0 -> x1, Pallas kernels: none -> 14.6 us  [shards(): pl.pallas_call(functools.partial(kernel, nz, nh), out_shape=jax.ShapeDtyp...]
    all_gather x1 -> x0, blocking collectives: 13.8 us -> none  [shards(): all_q = lax.all_gather(mine_q, 'grid', axis=0, tiled=True)]
    unnamed x6 -> x13, local copies, waits for them, and re-layouts: 1.49 us -> 5.79 us
    dot_general x8 -> x0, matrix products: 3.35 us -> none  [the longest x2 1.92 us: cache_terms(): jnp.einsum('qd,kd->qk', query, keys, preferred_element_type=jnp.float32)]
    reshape x2 -> x0, local copies, waits for them, and re-layouts: 1.36 us -> none  [the longest x1 0.68 us: shards(): tops.reshape(width, share, GROUP)]
    lt x1 -> x0, other arithmetic: 1.34 us -> none  [shards(): far = (key_pos < length)[None, :]]
  transfers between devices with their start and end apart: 6 -> 0, of which waited for: 4 -> 0; matrix products, arithmetic and copies ran while one was open for 15% -> 0% of each run, Pallas kernels for 0% -> 0%
where the time goes in v1:
time: 20.7 us; the launch traced here: 20.4 us
  Pallas kernels  14.6 us (71%)
  local copies, waits for them, and re-layouts  5.79 us (28%)
    pallas_call x1, Pallas kernels, shards(): pl.pallas_call(functools.partial(kernel, nz, nh), out_shape=jax.ShapeDtyp...  14.6 us
    unnamed x13, local copies, waits for them, and re-layouts  5.79 us

profile of v1, /device:TPU:0, one launch (start us, length us, event | category | flops | bytes accessed | tf_op | source)
XLA Modules:
  0.0 20.4 jit_solution(8494847038770405138)
XLA Ops:
  0.0 0.0 copy-start
  0.0 1.2 %copy-done = bf16[2,2048,128]{2,1,0:T(8,128)(2,1)S(1)} copy-done((bf16[2,2048,128]{2,1,0:T(8,128)(2,1)S(1)}, bf16[2,2048,128]{2,1,0:T(8,128)(2,1)}, u32[]{:S(2)}) %copy-start) | copy-done | bytes 1048600
  1.2 0.0 copy-start.1
  1.2 1.2 %copy-done.1 = bf16[2,2048,128]{2,1,0:T(8,128)(2,1)S(1)} copy-done((bf16[2,2048,128]{2,1,0:T(8,128)(2,1)S(1)}, bf16[2,2048,128]{2,1,0:T(8,128)(2,1)}, u32[]{:S(2)}) %copy-start.1) | copy-done | bytes 1048600
  2.5 0.0 copy-start.2
  2.5 0.7 %copy-done.2 = bf16[2,4096]{1,0:T(2,128)(2,1)S(1)} copy-done((bf16[2,4096]{1,0:T(2,128)(2,1)S(1)}, bf16[2,4096]{1,0:T(2,128)(2,1)}, u32[]{:S(2)}) %copy-start.2) | copy-done | bytes 16408
  3.2 0.0 copy-start.3
  3.2 0.7 %copy-done.3 = bf16[2,512]{1,0:T(2,128)(2,1)S(1)} copy-done((bf16[2,512]{1,0:T(2,128)(2,1)S(1)}, bf16[2,512]{1,0:T(2,128)(2,1)}, u32[]{:S(2)}) %copy-start.3) | copy-done | bytes 2072
  3.9 0.0 copy-start.4
  3.9 0.7 %copy-done.4 = bf16[2,512]{1,0:T(2,128)(2,1)S(1)} copy-done((bf16[2,512]{1,0:T(2,128)(2,1)S(1)}, bf16[2,512]{1,0:T(2,128)(2,1)}, u32[]{:S(2)}) %copy-start.4) | copy-done | bytes 2072
  4.5 0.0 copy-start.5
  4.5 0.7 %copy-done.5 = s32[2]{0:T(128)S(1)} copy-done((s32[2]{0:T(128)S(1)}, s32[2]{0:T(128)}, u32[]{:S(2)}) %copy-start.5) | copy-done | bytes 32
  5.2 14.6 %shard_map.64 = bf16[8,1024]{1,0:T(8,128)(2,1)S(1)} custom-call(bf16[2,4096]{1,0:T(2,128)(2,1)S(1)} %copy-done.2, bf16[2,2048,128]{2,1,0:T(8,128)(2,1)S(1)} %copy-done, bf16[2,2048,128]{2,1,0:T(8,128)(2,1)S(1)} %copy-done.1, bf16[2,512]{1,0:T(2,128)(2,1)S(1)} %copy-done.3, bf16[2,512]{1,0:T(2,128)(2,1)S(1)} %copy-done.4, s32[2]{0:T(128)S(1)} %copy-done.5), custom_call_target="tpu_custom_call" | custom-call | tf_op jit(solution)/shard_map/pallas_call | solution.py:249
  19.8 0.6 %copy.8 = bf16[8,1024]{1,0:T(8,128)(2,1)} copy(bf16[8,1024]{1,0:T(8,128)(2,1)S(1)} %shard_map.64) | data formatting | bytes 32768
Async XLA Ops:
  0.0 1.2 %copy-start = (bf16[2,2048,128]{2,1,0:T(8,128)(2,1)S(1)}, bf16[2,2048,128]{2,1,0:T(8,128)(2,1)}, u32[]{:S(2)}) copy-start(bf16[2,2048,128]{2,1,0:T(8,128)(2,1)} %k_in.1) | copy-start | bytes 3145732
  1.2 1.2 %copy-start.1 = (bf16[2,2048,128]{2,1,0:T(8,128)(2,1)S(1)}, bf16[2,2048,128]{2,1,0:T(8,128)(2,1)}, u32[]{:S(2)}) copy-start(bf16[2,2048,128]{2,1,0:T(8,128)(2,1)} %v_in.1) | copy-start | bytes 3145732
  2.5 0.7 %copy-start.2 = (bf16[2,4096]{1,0:T(2,128)(2,1)S(1)}, bf16[2,4096]{1,0:T(2,128)(2,1)}, u32[]{:S(2)}) copy-start(bf16[2,4096]{1,0:T(2,128)(2,1)} %q_in.1) | copy-start | bytes 49156
  3.2 0.7 %copy-start.3 = (bf16[2,512]{1,0:T(2,128)(2,1)S(1)}, bf16[2,512]{1,0:T(2,128)(2,1)}, u32[]{:S(2)}) copy-start(bf16[2,512]{1,0:T(2,128)(2,1)} %sk_in.1) | copy-start | bytes 6148
  3.9 0.7 %copy-start.4 = (bf16[2,512]{1,0:T(2,128)(2,1)S(1)}, bf16[2,512]{1,0:T(2,128)(2,1)}, u32[]{:S(2)}) copy-start(bf16[2,512]{1,0:T(2,128)(2,1)} %sv_in.1) | copy-start | bytes 6148
  4.5 0.7 %copy-start.5 = (s32[2]{0:T(128)S(1)}, s32[2]{0:T(128)}, u32[]{:S(2)}) copy-start(s32[2]{0:T(128)} %len_in.1) | copy-start | bytes 28

commit v2 on v1

--- a/solution.py
+++ b/solution.py
@@ -11,7 +11,7 @@
 HD = 128
 GROUP = 8
 REQS = 2
-PAD = 16
+NEAR = 128
 BLOCK_SRC = 8
 
 MASKED = -1e30
@@ -55,15 +55,14 @@
     nz, nh,
     q_in, k_in, v_in, sk_in, sv_in, len_in,
     out_ref,
-    q_own, sk_own, sv_own, lens, keys, values,
-    q_pack, kv_pack, q_msg, kv_msg, q_all, kv_all,
-    sum_msg, stat_msg, sum_all, stat_all, merged,
-    load_sem, cache_sem, q_send, q_recv, kv_send, kv_recv, sum_send, sum_recv, stat_send, stat_recv,
+    lens, keys, values, q_all, kv_all, near_pack,
+    sum_msg, stat_msg, sum_all, stat_all,
+    len_sem, cache_sem, q_send, q_recv, kv_send, kv_recv, sum_send, sum_recv, stat_send, stat_recv,
 ):
     n = nz * nh
     z, h = lax.axis_index("grid"), lax.axis_index("head")
     me = z * nh + h
-    local_rows = q_own.shape[0]
+    local_rows = sk_in.shape[1]
     msg_rows = local_rows * GROUP
     span = keys.shape[1]
     own_rows = local_rows * nh
@@ -85,14 +84,8 @@
 
     repeat(1, n, greet)
 
-    loads = [
-        pltpu.make_async_copy(q_in, q_own, load_sem.at[0]),
-        pltpu.make_async_copy(sk_in, sk_own, load_sem.at[1]),
-        pltpu.make_async_copy(sv_in, sv_own, load_sem.at[2]),
-        pltpu.make_async_copy(len_in, lens, load_sem.at[3]),
-    ]
-    for load in loads:
-        load.start()
+    len_load = pltpu.make_async_copy(len_in, lens, len_sem)
+    len_load.start()
     cache_loads = []
     for r in range(REQS):
         pair = (
@@ -103,61 +96,52 @@
             load.start()
         cache_loads.append(pair)
 
-    kv_pack[...] = jnp.zeros_like(kv_pack)
-    kv_all[nh:] = jnp.zeros((kv_all.shape[0] - nh,) + kv_all.shape[1:], BF16)
-    loads[0].wait()
-    q32 = q_own[...].astype(F32)
-    for oh in range(nh):
-        for j in range(GROUP):
-            column = (oh * GROUP + j) * HD
-            q_pack[pl.ds(oh * msg_rows + j, local_rows, stride=GROUP), :] = q32[:, column : column + HD]
-    q_msg[...] = q_pack[...].astype(BF16).reshape(q_msg.shape)
-    loads[1].wait()
-    loads[2].wait()
-    for t, own in enumerate((sk_own, sv_own)):
-        own32 = own[...].astype(F32)
-        for oh in range(nh):
-            kv_pack[pl.ds((oh * 2 + t) * PAD, local_rows), :] = own32[:, oh * HD : (oh + 1) * HD]
-    kv_msg[...] = kv_pack[...].astype(BF16).reshape(kv_msg.shape)
-
+    near_pack[...] = jnp.zeros_like(near_pack)
     pl.semaphore_wait(barrier, n - 1)
 
     def send_q(k):
         oz, oh = peer(k)
         pltpu.make_async_remote_copy(
-            src_ref=q_msg.at[oh], dst_ref=q_all.at[me], send_sem=q_send, recv_sem=q_recv.at[me // BLOCK_SRC],
+            src_ref=q_in.at[oh], dst_ref=q_all.at[me], send_sem=q_send, recv_sem=q_recv.at[me // BLOCK_SRC],
             device_id={"grid": oz, "head": oh}, device_id_type=MESH,
         ).start()
 
     repeat(1, n, send_q)
-    pltpu.make_async_copy(q_msg.at[h], q_all.at[me], q_recv.at[me // BLOCK_SRC]).start()
+    pltpu.make_async_copy(q_in.at[h], q_all.at[me], q_recv.at[me // BLOCK_SRC]).start()
     for k in range(1, nh):
         oh = lax.rem(h + k, nh)
-        pltpu.make_async_remote_copy(
-            src_ref=kv_msg.at[oh], dst_ref=kv_all.at[h], send_sem=kv_send, recv_sem=kv_recv,
-            device_id={"grid": z, "head": oh}, device_id_type=MESH,
-        ).start()
-    pltpu.make_async_copy(kv_msg.at[h], kv_all.at[h], kv_recv).start()
-
-    loads[3].wait()
+        for t, own in enumerate((sk_in, sv_in)):
+            pltpu.make_async_remote_copy(
+                src_ref=own.at[oh], dst_ref=kv_all.at[t, h], send_sem=kv_send, recv_sem=kv_recv,
+                device_id={"grid": z, "head": oh}, device_id_type=MESH,
+            ).start()
+    for t, own in enumerate((sk_in, sv_in)):
+        pltpu.make_async_copy(own.at[h], kv_all.at[t, h], kv_recv).start()
+
+    len_load.wait()
     unrolled = blocks <= 4
     if not unrolled:
         for pair in cache_loads:
             for load in pair:
                 load.wait()
-    landed = kv_all.at[pl.ds(0, nh)]
-    pltpu.make_async_copy(landed, landed, kv_recv).wait()
-    near_cols = kv_all.shape[0] * PAD
-    near_keys = kv_all[:, 0].reshape(near_cols, HD)
-    near_values = kv_all[:, 1].reshape(near_cols, HD)
+    pltpu.make_async_copy(kv_all, kv_all, kv_recv).wait()
+    for t in range(2):
+        for oh in range(nh):
+            near_pack[t, oh * local_rows : (oh + 1) * local_rows, :] = kv_all[t, oh].astype(F32)
+    near_keys = near_pack[0].astype(BF16)
+    near_values = near_pack[1].astype(BF16)
     key_pos = z * span + lax.broadcasted_iota(jnp.int32, (1, span), 1)
-    col = lax.broadcasted_iota(jnp.int32, (block_rows, near_cols), 1)
-    row = lax.broadcasted_iota(jnp.int32, (block_rows, near_cols), 0)
-    near_pos = z * own_rows + (col // PAD) * local_rows + col % PAD
-    near_real = (col % PAD < local_rows) & (col < nh * PAD)
+    col = lax.broadcasted_iota(jnp.int32, (block_rows, NEAR), 1)
+    row = lax.broadcasted_iota(jnp.int32, (block_rows, NEAR), 0)
+    near_pos = z * own_rows + col
+    near_real = col < own_rows
+    block_pos = row // msg_rows * local_rows + row % local_rows
     owner_row = lax.broadcasted_iota(jnp.int32, (owner_rows, 128), 0)
     owner_lane = lax.broadcasted_iota(jnp.int32, (owner_rows, 128), 1)
     diagonal = owner_lane % owner_rows == owner_row
+    out_pos = owner_row % own_rows
+    out_source = out_pos // local_rows * msg_rows + owner_row // own_rows * local_rows + out_pos % local_rows
+    out_diagonal = owner_lane % owner_rows == out_source
 
     def one_block(blk):
         first_row = blk * (block_rows // GROUP)
@@ -169,7 +153,7 @@
         pltpu.make_async_copy(q_all.at[sources], q_all.at[sources], q_recv.at[blk]).wait()
         query = q_all[sources].reshape(block_rows, HD)
         bias = jnp.where(key_pos < lens[request], 0.0, MASKED)
-        near_seen = near_real & (near_pos // per_req == request) & (near_pos <= first_row + row // GROUP)
+        near_seen = near_real & (near_pos // per_req == request) & (near_pos <= first_row + block_pos)
         top, total, summed = attend(query, keys[request], values[request], near_keys, near_values, bias, near_seen)
         summed = summed.astype(BF16)
         for o in range(owners):
@@ -216,19 +200,18 @@
         share = shares[b]
         for o in range(1, per_tile):
             share = jnp.where(owner_lane >= o * owner_rows, shares[b + o], share)
-        mix = jnp.where(diagonal, share, 0.0)
+        mix = jnp.where(out_diagonal, share, 0.0)
         high = mix.astype(BF16)
         low = (mix - high.astype(F32)).astype(BF16)
         sums = sum_all[pl.ds(b, per_tile)].reshape(per_tile * owner_rows, HD)
         acc = acc + jnp.dot(high, sums, preferred_element_type=F32)
         acc = acc + jnp.dot(low, sums, preferred_element_type=F32)
-    merged[...] = acc
     for j in range(GROUP):
-        out_ref[:, j * HD : (j + 1) * HD] = merged[pl.ds(j, own_rows, stride=GROUP), :].astype(BF16)
+        out_ref[:, j * HD : (j + 1) * HD] = acc[j * own_rows : (j + 1) * own_rows].astype(BF16)
 
     sent = q_all.at[pl.ds(0, n - 1)]
     pltpu.make_async_copy(sent, sent, q_send).wait()
-    sent = kv_all.at[pl.ds(0, nh - 1)]
+    sent = kv_all.at[:, pl.ds(0, nh - 1)]
     pltpu.make_async_copy(sent, sent, kv_send).wait()
     sent = stat_all.at[pl.ds(0, nz - 1)]
     pltpu.make_async_copy(sent, sent, stat_send).wait()
@@ -242,34 +225,29 @@
     local_rows = queries.shape[0]
     msg_rows = local_rows * GROUP
     owner_rows = local_rows * nh * GROUP
-    slots = -(-nh * PAD // 128) * 128 // PAD
+    queries = queries.reshape(local_rows, nh, GROUP, HD).transpose(1, 2, 0, 3).reshape(nh, msg_rows, HD)
+    stretch_keys = stretch_keys.reshape(local_rows, nh, HD).transpose(1, 0, 2)
+    stretch_values = stretch_values.reshape(local_rows, nh, HD).transpose(1, 0, 2)
     any_spec = pl.BlockSpec(memory_space=pl.ANY)
     vmem_spec = pl.BlockSpec(memory_space=pltpu.VMEM)
     dma = pltpu.SemaphoreType.DMA
     return pl.pallas_call(
         functools.partial(kernel, nz, nh),
-        out_shape=jax.ShapeDtypeStruct((local_rows * nh, GROUP * HD), BF16),
+        out_shape=pltpu.VMEM((local_rows * nh, GROUP * HD), BF16),
         in_specs=[any_spec] * 6,
         out_specs=vmem_spec,
         scratch_shapes=[
-            pltpu.VMEM(queries.shape, BF16),
-            pltpu.VMEM(stretch_keys.shape, BF16),
-            pltpu.VMEM(stretch_values.shape, BF16),
             pltpu.SMEM(cache_lengths.shape, jnp.int32),
             pltpu.VMEM(cache_keys.shape, BF16),
             pltpu.VMEM(cache_values.shape, BF16),
-            pltpu.VMEM((nh * msg_rows, HD), F32),
-            pltpu.VMEM((nh * 2 * PAD, HD), F32),
-            pltpu.VMEM((nh, msg_rows, HD), BF16),
-            pltpu.VMEM((nh, 2, PAD, HD), BF16),
             pltpu.VMEM((n, msg_rows, HD), BF16),
-            pltpu.VMEM((slots, 2, PAD, HD), BF16),
+            pltpu.VMEM((2, nh, local_rows, HD), BF16),
+            pltpu.VMEM((2, NEAR, HD), F32),
             pltpu.VMEM((nz, owner_rows, HD), BF16),
             pltpu.VMEM((nz, 2, 128), F32),
             pltpu.VMEM((nz, owner_rows, HD), BF16),
             pltpu.VMEM((nz, 2, 128), F32),
-            pltpu.VMEM((owner_rows, HD), F32),
-            dma((4,)),
+            dma,
             dma((2 * REQS,)),
             dma,
             dma((n // BLOCK_SRC,)),
@@ -281,7 +259,7 @@
             dma,
         ],
         compiler_params=pltpu.CompilerParams(
-            collective_id=0, has_side_effects=True, vmem_limit_bytes=48 * 1024 * 1024
+            collective_id=0, has_side_effects=True, vmem_limit_bytes=63 * 1024 * 1024
         ),
     )(queries, cache_keys, cache_values, stretch_keys, stretch_values, cache_lengths)
 

time: 20.7 us -> 15.5 us (0.75)
  local copies, waits for them, and re-layouts: 5.79 us -> 0.61 us
    unnamed x13 -> x1, local copies, waits for them, and re-layouts: 5.79 us -> 0.61 us
where the time goes in v2:
time: 15.5 us; the launch traced here: 15.4 us
  Pallas kernels  14.8 us (95%)
  local copies, waits for them, and re-layouts  0.61 us (4%)
    pallas_call x1, Pallas kernels, shards(): pl.pallas_call(functools.partial(kernel, nz, nh), out_shape=pltpu.VMEM((l...  14.8 us
    unnamed x1, local copies, waits for them, and re-layouts  0.61 us

profile of v2, /device:TPU:0, one launch (start us, length us, event | category | flops | bytes accessed | tf_op | source)
XLA Modules:
  0.0 15.4 jit_solution(4840419895188324326)
XLA Ops:
  0.0 14.8 %shard_map.64 = bf16[8,1024]{1,0:T(8,128)(2,1)S(1)} custom-call(bf16[4,16,128]{2,1,0:T(8,128)(2,1)} %bitcast.11, bf16[2,2048,128]{2,1,0:T(8,128)(2,1)} %k_in.1, bf16[2,2048,128]{2,1,0:T(8,128)(2,1)} %v_in.1, bf16[4,2,128]{2,1,0:T(2,128)(2,1)} %bitcast.12, bf16[4,2,128]{2,1,0:T(2,128)(2,1)} %bitcast.13, s32[2]{0:T(128)} %len_in.1), custom_call_target="tpu_custom_call" | custom-call | tf_op jit(solution)/shard_map/pallas_call | solution.py:234
  14.8 0.6 %copy.9 = bf16[8,1024]{1,0:T(8,128)(2,1)} copy(bf16[8,1024]{1,0:T(8,128)(2,1)S(1)} %shard_map.64) | data formatting | bytes 32768

commit v3 on v2

--- a/solution.py
+++ b/solution.py
@@ -55,9 +55,9 @@
     nz, nh,
     q_in, k_in, v_in, sk_in, sv_in, len_in,
     out_ref,
-    lens, keys, values, q_all, kv_all, near_pack,
+    q_own, sk_own, sv_own, lens, keys, values, q_all, kv_all, near_pack,
     sum_msg, stat_msg, sum_all, stat_all,
-    len_sem, cache_sem, q_send, q_recv, kv_send, kv_recv, sum_send, sum_recv, stat_send, stat_recv,
+    load_sem, cache_sem, q_send, q_recv, kv_send, kv_recv, sum_send, sum_recv, stat_send, stat_recv,
 ):
     n = nz * nh
     z, h = lax.axis_index("grid"), lax.axis_index("head")
@@ -72,20 +72,28 @@
     blocks = n // BLOCK_SRC
     owners = block_rows // owner_rows
 
+    def wrapped(index, size):
+        return jnp.where(index >= size, index - size, index)
+
     def peer(k):
-        other = lax.rem(me + k, n)
-        return other // nh, lax.rem(other, nh)
+        other = n - k
+        other = jnp.where(other <= me, other - 1, other)
+        return lax.div(other, nh), lax.rem(other, nh)
 
     barrier = pltpu.get_barrier_semaphore()
 
     def greet(k):
-        oz, oh = peer(k)
+        oz, oh = peer(n - k)
         pl.semaphore_signal(barrier, inc=1, device_id={"grid": oz, "head": oh}, device_id_type=MESH)
 
     repeat(1, n, greet)
 
-    len_load = pltpu.make_async_copy(len_in, lens, len_sem)
-    len_load.start()
+    loads = [
+        pltpu.make_async_copy(source, own, load_sem.at[i])
+        for i, (source, own) in enumerate(((q_in, q_own), (sk_in, sk_own), (sv_in, sv_own), (len_in, lens)))
+    ]
+    for load in loads:
+        load.start()
     cache_loads = []
     for r in range(REQS):
         pair = (
@@ -97,28 +105,30 @@
         cache_loads.append(pair)
 
     near_pack[...] = jnp.zeros_like(near_pack)
+    for load in loads[:3]:
+        load.wait()
     pl.semaphore_wait(barrier, n - 1)
 
     def send_q(k):
         oz, oh = peer(k)
         pltpu.make_async_remote_copy(
-            src_ref=q_in.at[oh], dst_ref=q_all.at[me], send_sem=q_send, recv_sem=q_recv.at[me // BLOCK_SRC],
+            src_ref=q_own.at[oh], dst_ref=q_all.at[me], send_sem=q_send, recv_sem=q_recv.at[me // BLOCK_SRC],
             device_id={"grid": oz, "head": oh}, device_id_type=MESH,
         ).start()
 
     repeat(1, n, send_q)
-    pltpu.make_async_copy(q_in.at[h], q_all.at[me], q_recv.at[me // BLOCK_SRC]).start()
+    pltpu.make_async_copy(q_own.at[h], q_all.at[me], q_recv.at[me // BLOCK_SRC]).start()
     for k in range(1, nh):
-        oh = lax.rem(h + k, nh)
-        for t, own in enumerate((sk_in, sv_in)):
+        oh = wrapped(h + k, nh)
+        for t, own in enumerate((sk_own, sv_own)):
             pltpu.make_async_remote_copy(
                 src_ref=own.at[oh], dst_ref=kv_all.at[t, h], send_sem=kv_send, recv_sem=kv_recv,
                 device_id={"grid": z, "head": oh}, device_id_type=MESH,
             ).start()
-    for t, own in enumerate((sk_in, sv_in)):
+    for t, own in enumerate((sk_own, sv_own)):
         pltpu.make_async_copy(own.at[h], kv_all.at[t, h], kv_recv).start()
 
-    len_load.wait()
+    loads[3].wait()
     unrolled = blocks <= 4
     if not unrolled:
         for pair in cache_loads:
@@ -143,17 +153,24 @@
     out_source = out_pos // local_rows * msg_rows + owner_row // own_rows * local_rows + out_pos % local_rows
     out_diagonal = owner_lane % owner_rows == out_source
 
-    def one_block(blk):
+    def masks(blk):
         first_row = blk * (block_rows // GROUP)
         request = first_row // per_req
+        bias = jnp.where(key_pos < lens[request], 0.0, MASKED)
+        near_seen = near_real & (near_pos // per_req == request) & (near_pos <= first_row + block_pos)
+        return request, bias, near_seen
+
+    ready = [masks(blk) for blk in range(blocks)] if unrolled else None
+
+    def one_block(blk):
+        request, bias, near_seen = ready[blk] if unrolled else masks(blk)
+        first_row = blk * (block_rows // GROUP)
         sources = pl.ds(blk * BLOCK_SRC, BLOCK_SRC)
         if unrolled and first_row % per_req == 0:
             for load in cache_loads[request]:
                 load.wait()
         pltpu.make_async_copy(q_all.at[sources], q_all.at[sources], q_recv.at[blk]).wait()
         query = q_all[sources].reshape(block_rows, HD)
-        bias = jnp.where(key_pos < lens[request], 0.0, MASKED)
-        near_seen = near_real & (near_pos // per_req == request) & (near_pos <= first_row + block_pos)
         top, total, summed = attend(query, keys[request], values[request], near_keys, near_values, bias, near_seen)
         summed = summed.astype(BF16)
         for o in range(owners):
@@ -237,6 +254,9 @@
         in_specs=[any_spec] * 6,
         out_specs=vmem_spec,
         scratch_shapes=[
+            pltpu.VMEM(queries.shape, BF16),
+            pltpu.VMEM(stretch_keys.shape, BF16),
+            pltpu.VMEM(stretch_values.shape, BF16),
             pltpu.SMEM(cache_lengths.shape, jnp.int32),
             pltpu.VMEM(cache_keys.shape, BF16),
             pltpu.VMEM(cache_values.shape, BF16),
@@ -247,7 +267,7 @@
             pltpu.VMEM((nz, 2, 128), F32),
             pltpu.VMEM((nz, owner_rows, HD), BF16),
             pltpu.VMEM((nz, 2, 128), F32),
-            dma,
+            dma((4,)),
             dma((2 * REQS,)),
             dma,
             dma((n // BLOCK_SRC,)),

time: 15.5 us -> 15.2 us (0.981)
  Pallas kernels: 14.8 us -> 14.4 us
    pallas_call x1, Pallas kernels: 14.8 us -> 14.4 us  [shards(): pl.pallas_call(functools.partial(kernel, nz, nh), out_shape=pltpu.VMEM((l...]
where the time goes in v3:
time: 15.2 us; the launch traced here: 15 us
  Pallas kernels  14.4 us (95%)
  local copies, waits for them, and re-layouts  0.61 us (4%)
    pallas_call x1, Pallas kernels, shards(): pl.pallas_call(functools.partial(kernel, nz, nh), out_shape=pltpu.VMEM((l...  14.4 us
    unnamed x1, local copies, waits for them, and re-layouts  0.61 us

profile of v3, /device:TPU:0, one launch (start us, length us, event | category | flops | bytes accessed | tf_op | source)
XLA Modules:
  0.0 15.0 jit_solution(7970372504395279683)
XLA Ops:
  0.0 14.4 %shard_map.64 = bf16[8,1024]{1,0:T(8,128)(2,1)S(1)} custom-call(bf16[4,16,128]{2,1,0:T(8,128)(2,1)} %bitcast.11, bf16[2,2048,128]{2,1,0:T(8,128)(2,1)} %k_in.1, bf16[2,2048,128]{2,1,0:T(8,128)(2,1)} %v_in.1, bf16[4,2,128]{2,1,0:T(2,128)(2,1)} %bitcast.12, bf16[4,2,128]{2,1,0:T(2,128)(2,1)} %bitcast.13, s32[2]{0:T(128)} %len_in.1), custom_call_target="tpu_custom_call" | custom-call | tf_op jit(solution)/shard_map/pallas_call | solution.py:251
  14.4 0.6 %copy.9 = bf16[8,1024]{1,0:T(8,128)(2,1)} copy(bf16[8,1024]{1,0:T(8,128)(2,1)S(1)} %shard_map.64) | data formatting | bytes 32768

commit v4 on v3

--- a/solution.py
+++ b/solution.py
@@ -12,6 +12,7 @@
 GROUP = 8
 REQS = 2
 NEAR = 128
+CHUNK = 512
 BLOCK_SRC = 8
 
 MASKED = -1e30
@@ -38,16 +39,28 @@
 
 def attend(query, keys, values, near_keys, near_values, bias, near_seen):
     contract = (((1,), (1,)), ((), ()))
-    scores = lax.dot_general(query, keys, contract, preferred_element_type=F32) + bias
+    span = keys.shape[0]
+    chunk = math.gcd(span, CHUNK)
+    parts = [slice(c, c + chunk) for c in range(0, span, chunk)]
     near = lax.dot_general(query, near_keys, contract, preferred_element_type=F32)
     near = jnp.where(near_seen, near, MASKED)
-    top = jnp.maximum(jnp.max(scores, axis=1, keepdims=True), jnp.max(near, axis=1, keepdims=True))
-    top = jnp.maximum(top, FLOOR)
-    weights = jnp.exp2((scores - top) * LOG2_SCALE)
+    scores = [
+        lax.dot_general(query, keys[part], contract, preferred_element_type=F32) + bias[:, part] for part in parts
+    ]
+    lanes = near
+    for score in scores:
+        for c in range(0, chunk, NEAR):
+            lanes = jnp.maximum(lanes, score[:, c : c + NEAR])
+    top = jnp.maximum(jnp.max(lanes, axis=1, keepdims=True), FLOOR)
     near_w = jnp.exp2((near - top) * LOG2_SCALE)
-    total = jnp.sum(weights, axis=1, keepdims=True) + jnp.sum(near_w, axis=1, keepdims=True)
-    summed = jnp.dot(weights.astype(BF16), values, preferred_element_type=F32)
-    summed = summed + jnp.dot(near_w.astype(BF16), near_values, preferred_element_type=F32)
+    lanes = near_w
+    summed = jnp.dot(near_w.astype(BF16), near_values, preferred_element_type=F32)
+    for part, score in zip(parts, scores):
+        weights = jnp.exp2((score - top) * LOG2_SCALE)
+        for c in range(0, chunk, NEAR):
+            lanes = lanes + weights[:, c : c + NEAR]
+        summed = summed + jnp.dot(weights.astype(BF16), values[part], preferred_element_type=F32)
+    total = jnp.sum(lanes, axis=1, keepdims=True)
     return top, total, summed
 
 

time: 15.2 us -> 15.2 us (level)
  no operation moved by 1% of the time
where the time goes in v4:
time: 15.2 us; the launch traced here: 15 us
  Pallas kernels  14.4 us (95%)
  local copies, waits for them, and re-layouts  0.61 us (4%)
    pallas_call x1, Pallas kernels, shards(): pl.pallas_call(functools.partial(kernel, nz, nh), out_shape=pltpu.VMEM((l...  14.4 us
    unnamed x1, local copies, waits for them, and re-layouts  0.61 us

profile of v4, /device:TPU:0, one launch (start us, length us, event | category | flops | bytes accessed | tf_op | source)
XLA Modules:
  0.0 15.0 jit_solution(12552565935194560344)
XLA Ops:
  0.0 14.4 %shard_map.64 = bf16[8,1024]{1,0:T(8,128)(2,1)S(1)} custom-call(bf16[4,16,128]{2,1,0:T(8,128)(2,1)} %bitcast.11, bf16[2,2048,128]{2,1,0:T(8,128)(2,1)} %k_in.1, bf16[2,2048,128]{2,1,0:T(8,128)(2,1)} %v_in.1, bf16[4,2,128]{2,1,0:T(2,128)(2,1)} %bitcast.12, bf16[4,2,128]{2,1,0:T(2,128)(2,1)} %bitcast.13, s32[2]{0:T(128)} %len_in.1), custom_call_target="tpu_custom_call" | custom-call | tf_op jit(solution)/shard_map/pallas_call | solution.py:264
  14.4 0.6 %copy.9 = bf16[8,1024]{1,0:T(8,128)(2,1)} copy(bf16[8,1024]{1,0:T(8,128)(2,1)S(1)} %shard_map.64) | data formatting | bytes 32768
